TPU v7x, 32 devices: a whole 2x2x4 slice. The times are simulated.
32 devices in a mesh: groups: 2 (over y), resp: 8 (over z, x), mp: 2 (over core).
Axes of the slice: x: 2, y: 2, z: 4, core: 2. Of those that a mesh axis runs over, the one named last changes fastest.
Arguments:
- query: bfloat16 [2048, 4096], P(('groups', 'resp'), 'mp'), parts along dimension 0, may hold values from -8 to 8
- saved_out: bfloat16 [2048, 4096], P(('groups', 'resp'), 'mp'), parts along dimension 0, may hold values from -6 to 6
- d_out: bfloat16 [2048, 4096], P(('groups', 'resp'), 'mp'), parts along dimension 0, may hold values from -48 to 48
- resp_kv: bfloat16 [2, 2048, 512], P(None, ('groups', 'resp'), 'mp'), parts along dimension 1, may hold values from -6 to 6
- prompt_kv: bfloat16 [2, 2048, 512], P(None, ('groups', 'resp'), 'mp'), parts along dimension 1, may hold values from -8 to 8
- prefix_blocks: int32 [16], P(('groups', 'resp')), parts along dimension 0, may hold values from 1 to 8, as said below
- resp_len: int32 [16], P(('groups', 'resp')), parts along dimension 0, may hold values from 1 to 128, as said below
- block_position: int32 [16], P(('groups', 'resp')), parts along dimension 0, may hold values from 0 to 7, as said below
Outputs:
- d_query: bfloat16 [2048, 4096], P(('groups', 'resp'), 'mp'), parts along dimension 0
- d_resp_kv: bfloat16 [2, 2048, 512], P(None, ('groups', 'resp'), 'mp'), parts along dimension 1
- d_prompt_kv: bfloat16 [2, 2048, 512], P(None, ('groups', 'resp'), 'mp'), parts along dimension 1
There are 2 independent parts, one for each index of `groups`. A program takes and returns all parts, laid end to end along the dimension named above; each array names one. Nothing has to cross between parts.
Inputs may be any that keep to these rules, and one draw needn't show every extreme that they name: `prefix_blocks`: some response sees all 8 blocks of its prompt. `resp_len`: some response has all 128 tokens live. `block_position`: for each prompt c, the entries c, c + 1, c + 2, ... hold every position 0 to 7 once.
All inputs are finite; a program needn't handle non-finite values.
Results may differ from a plain program's by a relative error of at most 0.0051.
Values may be sent and summed in bfloat16 or wider, within the bound.
A program may use at most 64 MiB of HBM per device.

v0:
```python
import jax
import jax.numpy as jnp
from jax import lax
from jax.sharding import PartitionSpec as P

HD = 128


blocked_score = -1e30


def passed_along(array, axis, by):
    count = lax.axis_size(axis)
    return lax.ppermute(array, axis, [(i, (i + by) % count) for i in range(count)])


def on_device(query, saved_out, d_out, resp_kv, prompt_kv, prefix_blocks, resp_len, block_position):
    row_count = query.shape[0]
    kv_heads = resp_kv.shape[2] // HD
    head_count = query.shape[1] // HD
    ratio = head_count // kv_heads
    block_rows = prompt_kv.shape[1]
    feature_width = resp_kv.shape[2]
    axis_total = lax.axis_size("resp")
    group_size = min(16, axis_total)
    stride = axis_total // group_size
    group_place = lax.axis_index("resp") // stride
    score_scale = HD ** (-0.5)
    visible_count = prefix_blocks[0]
    queries = query.reshape(row_count, kv_heads, ratio, HD)
    row_index = jnp.arange(row_count)
    alive_rows = row_index < resp_len[0]
    causal = row_index[:, None] >= row_index[None, :]
    grads = jnp.where(alive_rows[:, None], d_out, jnp.zeros_like(d_out))
    grads_heads = grads.reshape(row_count, kv_heads, ratio, HD)
    delta = jnp.sum(
        grads.astype(jnp.float32).reshape(row_count, kv_heads, ratio, HD)
        * saved_out.astype(jnp.float32).reshape(row_count, kv_heads, ratio, HD),
        axis=3,
    )
    delta = jnp.transpose(delta, (1, 2, 0))

    def logits(key_flat):
        key_rows = key_flat.reshape(-1, kv_heads, HD)
        return (
            jnp.einsum("rgjd,tgd->gjrt", queries, key_rows, preferred_element_type=jnp.float32)
            * score_scale
        )

    def update(state, kv_block, allowed):
        running_max, running_sum = state
        scores = jnp.where(allowed, logits(kv_block[0]), blocked_score)
        new_max = jnp.maximum(running_max, jnp.max(scores, axis=-1))
        running_sum = running_sum * jnp.exp(running_max - new_max) + jnp.sum(
            jnp.exp(scores - new_max[..., None]), axis=-1
        )
        return (new_max, running_sum)

    def fold_block(state, kv_block, position):
        return update(state, kv_block, position < visible_count)

    local_scores = jnp.where(causal, logits(resp_kv[0]), blocked_score)
    start_max = jnp.max(local_scores, axis=-1)
    state = (start_max, jnp.sum(jnp.exp(local_scores - start_max[..., None]), axis=-1))
    stash = jnp.zeros((group_size,) + prompt_kv.shape, jnp.bfloat16)
    stash = lax.dynamic_update_index_in_dim(stash, prompt_kv, group_place, 0)
    stash_pos = jnp.zeros((group_size,), jnp.int32)
    stash_pos = lax.dynamic_update_index_in_dim(stash_pos, block_position[0], group_place, 0)
    state = fold_block(state, prompt_kv, block_position[0])

    def forward_turn(turn_index, carry):
        kv_block, position, stash, stash_pos, running_max, running_sum = carry
        kv_block, position = passed_along((kv_block, position), "resp", stride)
        source = (group_place - turn_index) % group_size
        stash = lax.dynamic_update_index_in_dim(stash, kv_block, source, 0)
        stash_pos = lax.dynamic_update_index_in_dim(stash_pos, position[0], source, 0)
        running_max, running_sum = fold_block((running_max, running_sum), kv_block, position[0])
        return (kv_block, position, stash, stash_pos, running_max, running_sum)

    carry = lax.fori_loop(
        1,
        group_size,
        forward_turn,
        (prompt_kv, block_position, stash, stash_pos, state[0], state[1]),
    )
    stash, stash_pos = (carry[2], carry[3])
    state = (carry[4], carry[5])
    log_total = state[0] + jnp.log(state[1])

    def backward_part(kv_block, allowed):
        key_rows = kv_block[0].reshape(-1, kv_heads, HD)
        value_rows = kv_block[1].reshape(-1, kv_heads, HD)
        scores = logits(kv_block[0])
        weights = jnp.where(allowed, jnp.exp(scores - log_total[..., None]), 0.0)
        weights_low = weights.astype(jnp.bfloat16)
        value_grad = jnp.einsum(
            "gjrt,rgjd->tgd", weights_low, grads_heads, preferred_element_type=jnp.float32
        )
        weight_grad = jnp.einsum(
            "rgjd,tgd->gjrt", grads_heads, value_rows, preferred_element_type=jnp.float32
        )
        score_grad = (weights * (weight_grad - delta[..., None]) * score_scale).astype(jnp.bfloat16)
        query_grad = jnp.einsum(
            "gjrt,tgd->rgjd", score_grad, key_rows, preferred_element_type=jnp.float32
        )
        key_grad = jnp.einsum(
            "gjrt,rgjd->tgd", score_grad, queries, preferred_element_type=jnp.float32
        )
        return (query_grad, jnp.stack([key_grad, value_grad]).reshape(2, -1, feature_width))

    empty_block = jnp.zeros((2, block_rows, feature_width), jnp.float32)

    def back_block(kv_block, position):
        return backward_part(kv_block, position < visible_count)

    query_grad, local_grad = backward_part(resp_kv, causal)

    def backward_turn(turn_index, carry):
        partial_value, query_total = carry
        source = (group_place - 1 - turn_index) % group_size
        part_query, part_block = back_block(stash[source], stash_pos[source])
        moved = passed_along(partial_value + part_block, "resp", stride)
        return (moved, query_total + part_query)

    partial_value, query_grad = lax.fori_loop(
        0, group_size - 1, backward_turn, (empty_block, query_grad)
    )
    part_query, part_block = back_block(stash[group_place], stash_pos[group_place])
    prompt_grad = partial_value + part_block
    query_grad = query_grad + part_query
    d_query = query_grad.reshape(row_count, head_count * HD).astype(jnp.bfloat16)
    return (d_query, local_grad.astype(jnp.bfloat16), prompt_grad.astype(jnp.bfloat16))


def solution(mesh):
    placed = (
        P(("groups", "resp"), "mp"),
        P(("groups", "resp"), "mp"),
        P(("groups", "resp"), "mp"),
        P(None, ("groups", "resp"), "mp"),
        P(None, ("groups", "resp"), "mp"),
        P(("groups", "resp")),
        P(("groups", "resp")),
        P(("groups", "resp")),
    )
    return jax.shard_map(
        on_device,
        mesh=mesh,
        in_specs=placed,
        out_specs=(
            P(("groups", "resp"), "mp"),
            P(None, ("groups", "resp"), "mp"),
            P(None, ("groups", "resp"), "mp"),
        ),
        check_vma=False,
    )
```

profile of v0, /device:TPU:0, one launch (start us, length us, event | category | flops | bytes accessed | tf_op | source)
XLA Modules:
  0.0 210.4 jit_solution(18338941951631233019)
XLA Ops:
  2.8 1.0 copy.97
  4.5 0.9 fusion.41
  5.5 0.7 copy.177
  7.9 0.7 copy-done.4
  9.4 79.1 %while.42 = (s32[]{:T(128)}, bf16[2,128,256]{1,2,0:T(8,128)(2,1)S(1)}, s32[1]{0:T(128)}, bf16[8,2,128,256]{2,3,1,0:T(8,128)(2,1)S(1)}, s32[8]{0:T(128)S(1)}, /*i...) while((s32[]{:T(128)}, ...), condition=%wide.region_7.8_spmd, body=%wide.region_4.7_spmd.sunk | while | flops 68685840 | bytes 3973539 | solution.py:80
  9.5 3.0 %collective-permute-start = (bf16[2,128,256]{1,2,0:T(8,128)(2,1)S(1)}, bf16[2,128,256]{1,2,0:T(8,128)(2,1)S(1)}, u32[]{:S(2)}, u32[]{:S(2)}) collective-permute-start(bf16[2,128,256]{1,2,0:T(8,128)(2,1)S(1)} %get-tuple-element.805), channel_id=1, source_target_pairs={{0,2},{2,4},{4,6},{6,8},{8,10},{10,12},{12,14},{14,0},{1,3},{3,5},... | collective-permute-start | bytes 393224 | tf_op jit(solution)/shard_map/while/body/eval_jaxpr/ppermute | solution.py:14
  12.5 2.8 %collective-permute-start.1 = (s32[1]{0:T(128)}, s32[1]{0:T(128)}, u32[]{:S(2)}, u32[]{:S(2)}) collective-permute-start(s32[1]{0:T(128)} %copy.192), channel_id=1, source_target_pairs={{0,2},{2,4},{4,6},{6,8},{8,10},{10,12},{12,14},{14,0},{1,3},{3,5},... | collective-permute-start | bytes 20 | tf_op jit(solution)/shard_map/while/body/eval_jaxpr/ppermute | solution.py:14
  15.3 3.9 %collective-permute-done.1 = s32[1]{0:T(128)} collective-permute-done((s32[1]{0:T(128)}, s32[1]{0:T(128)}, u32[]{:S(2)}, u32[]{:S(2)}) %collective-permute-start.1) | collective-permute-done | bytes 36 | tf_op jit(solution)/shard_map/while/body/eval_jaxpr/ppermute | solution.py:14
  22.4 2.6 %collective-permute-start.1 = (s32[1]{0:T(128)}, s32[1]{0:T(128)}, u32[]{:S(2)}, u32[]{:S(2)}) collective-permute-start(s32[1]{0:T(128)} %copy.192), channel_id=1, source_target_pairs={{0,2},{2,4},{4,6},{6,8},{8,10},{10,12},{12,14},{14,0},{1,3},{3,5},... | collective-permute-start | bytes 20 | tf_op jit(solution)/shard_map/while/body/eval_jaxpr/ppermute | solution.py:14
  24.9 5.3 %collective-permute-done.1 = s32[1]{0:T(128)} collective-permute-done((s32[1]{0:T(128)}, s32[1]{0:T(128)}, u32[]{:S(2)}, u32[]{:S(2)}) %collective-permute-start.1) | collective-permute-done | bytes 36 | tf_op jit(solution)/shard_map/while/body/eval_jaxpr/ppermute | solution.py:14
  33.4 2.6 %collective-permute-start.1 = (s32[1]{0:T(128)}, s32[1]{0:T(128)}, u32[]{:S(2)}, u32[]{:S(2)}) collective-permute-start(s32[1]{0:T(128)} %copy.192), channel_id=1, source_target_pairs={{0,2},{2,4},{4,6},{6,8},{8,10},{10,12},{12,14},{14,0},{1,3},{3,5},... | collective-permute-start | bytes 20 | tf_op jit(solution)/shard_map/while/body/eval_jaxpr/ppermute | solution.py:14
  36.0 5.3 %collective-permute-done.1 = s32[1]{0:T(128)} collective-permute-done((s32[1]{0:T(128)}, s32[1]{0:T(128)}, u32[]{:S(2)}, u32[]{:S(2)}) %collective-permute-start.1) | collective-permute-done | bytes 36 | tf_op jit(solution)/shard_map/while/body/eval_jaxpr/ppermute | solution.py:14
  44.4 2.6 %collective-permute-start.1 = (s32[1]{0:T(128)}, s32[1]{0:T(128)}, u32[]{:S(2)}, u32[]{:S(2)}) collective-permute-start(s32[1]{0:T(128)} %copy.192), channel_id=1, source_target_pairs={{0,2},{2,4},{4,6},{6,8},{8,10},{10,12},{12,14},{14,0},{1,3},{3,5},... | collective-permute-start | bytes 20 | tf_op jit(solution)/shard_map/while/body/eval_jaxpr/ppermute | solution.py:14
  47.0 5.3 %collective-permute-done.1 = s32[1]{0:T(128)} collective-permute-done((s32[1]{0:T(128)}, s32[1]{0:T(128)}, u32[]{:S(2)}, u32[]{:S(2)}) %collective-permute-start.1) | collective-permute-done | bytes 36 | tf_op jit(solution)/shard_map/while/body/eval_jaxpr/ppermute | solution.py:14
  55.5 2.6 %collective-permute-start.1 = (s32[1]{0:T(128)}, s32[1]{0:T(128)}, u32[]{:S(2)}, u32[]{:S(2)}) collective-permute-start(s32[1]{0:T(128)} %copy.192), channel_id=1, source_target_pairs={{0,2},{2,4},{4,6},{6,8},{8,10},{10,12},{12,14},{14,0},{1,3},{3,5},... | collective-permute-start | bytes 20 | tf_op jit(solution)/shard_map/while/body/eval_jaxpr/ppermute | solution.py:14
  58.0 5.3 %collective-permute-done.1 = s32[1]{0:T(128)} collective-permute-done((s32[1]{0:T(128)}, s32[1]{0:T(128)}, u32[]{:S(2)}, u32[]{:S(2)}) %collective-permute-start.1) | collective-permute-done | bytes 36 | tf_op jit(solution)/shard_map/while/body/eval_jaxpr/ppermute | solution.py:14
  66.5 2.6 %collective-permute-start.1 = (s32[1]{0:T(128)}, s32[1]{0:T(128)}, u32[]{:S(2)}, u32[]{:S(2)}) collective-permute-start(s32[1]{0:T(128)} %copy.192), channel_id=1, source_target_pairs={{0,2},{2,4},{4,6},{6,8},{8,10},{10,12},{12,14},{14,0},{1,3},{3,5},... | collective-permute-start | bytes 20 | tf_op jit(solution)/shard_map/while/body/eval_jaxpr/ppermute | solution.py:14
  69.1 5.3 %collective-permute-done.1 = s32[1]{0:T(128)} collective-permute-done((s32[1]{0:T(128)}, s32[1]{0:T(128)}, u32[]{:S(2)}, u32[]{:S(2)}) %collective-permute-start.1) | collective-permute-done | bytes 36 | tf_op jit(solution)/shard_map/while/body/eval_jaxpr/ppermute | solution.py:14
  77.5 2.6 %collective-permute-start.1 = (s32[1]{0:T(128)}, s32[1]{0:T(128)}, u32[]{:S(2)}, u32[]{:S(2)}) collective-permute-start(s32[1]{0:T(128)} %copy.192), channel_id=1, source_target_pairs={{0,2},{2,4},{4,6},{6,8},{8,10},{10,12},{12,14},{14,0},{1,3},{3,5},... | collective-permute-start | bytes 20 | tf_op jit(solution)/shard_map/while/body/eval_jaxpr/ppermute | solution.py:14
  80.1 5.3 %collective-permute-done.1 = s32[1]{0:T(128)} collective-permute-done((s32[1]{0:T(128)}, s32[1]{0:T(128)}, u32[]{:S(2)}, u32[]{:S(2)}) %collective-permute-start.1) | collective-permute-done | bytes 36 | tf_op jit(solution)/shard_map/while/body/eval_jaxpr/ppermute | solution.py:14
  91.5 1.0 multiply_bitcast_fusion
  92.5 1.2 copy.178
  93.7 1.6 reduce_sum.45
  95.4 1.3 copy.99
  96.8 1.0 fusion.31
  97.8 1.2 fusion.29
  99.0 0.9 copy.117
  100.0 1.3 fusion.30
  102.8 0.8 copy.121
  103.9 0.8 copy.120
  105.9 100.5 %while.43 = (s32[]{:T(128)}, f32[2,128,256]{1,2,0:T(8,128)S(1)}, f32[128,2,8,128]{0,3,2,1:T(8,128)S(1)}, s32[]{:T(128)}, s32[8]{0:T(128)S(1)}, /*index=5*/s32[]{...) while((s32[]{:T(128)}, f32[2,128,256]{1,2,0:T(8,128)S(1)}, ...), condition=%wide.region_10.11_spmd, body=%wide.region_9.10_spmd.sunk | while | flops 338034688 | bytes 11485570 | solution.py:125
  107.8 0.9 constant_dynamic-slice_fusion.5
  110.5 9.0 %collective-permute-done.2 = f32[2,128,256]{1,2,0:T(8,128)S(1)} collective-permute-done((f32[2,128,256]{1,2,0:T(8,128)S(1)}, f32[2,128,256]{1,2,0:T(8,128)S(1)}, u32[]{:S(2)}, u32[]{:S(2)}) %collective-permute-start.2) | collective-permute-done | bytes 262176 | tf_op jit(solution)/shard_map/while/body/eval_jaxpr/ppermute | solution.py:14
  121.4 0.9 constant_dynamic-slice_fusion.5
  124.1 10.1 %collective-permute-done.2 = f32[2,128,256]{1,2,0:T(8,128)S(1)} collective-permute-done((f32[2,128,256]{1,2,0:T(8,128)S(1)}, f32[2,128,256]{1,2,0:T(8,128)S(1)}, u32[]{:S(2)}, u32[]{:S(2)}) %collective-permute-start.2) | collective-permute-done | bytes 262176 | tf_op jit(solution)/shard_map/while/body/eval_jaxpr/ppermute | solution.py:14
  136.0 0.9 constant_dynamic-slice_fusion.5
  138.7 11.2 %collective-permute-done.2 = f32[2,128,256]{1,2,0:T(8,128)S(1)} collective-permute-done((f32[2,128,256]{1,2,0:T(8,128)S(1)}, f32[2,128,256]{1,2,0:T(8,128)S(1)}, u32[]{:S(2)}, u32[]{:S(2)}) %collective-permute-start.2) | collective-permute-done | bytes 262176 | tf_op jit(solution)/shard_map/while/body/eval_jaxpr/ppermute | solution.py:14
  151.8 0.9 constant_dynamic-slice_fusion.5
  154.5 10.7 %collective-permute-done.2 = f32[2,128,256]{1,2,0:T(8,128)S(1)} collective-permute-done((f32[2,128,256]{1,2,0:T(8,128)S(1)}, f32[2,128,256]{1,2,0:T(8,128)S(1)}, u32[]{:S(2)}, u32[]{:S(2)}) %collective-permute-start.2) | collective-permute-done | bytes 262176 | tf_op jit(solution)/shard_map/while/body/eval_jaxpr/ppermute | solution.py:14
  167.1 0.9 constant_dynamic-slice_fusion.5
  169.8 9.9 %collective-permute-done.2 = f32[2,128,256]{1,2,0:T(8,128)S(1)} collective-permute-done((f32[2,128,256]{1,2,0:T(8,128)S(1)}, f32[2,128,256]{1,2,0:T(8,128)S(1)}, u32[]{:S(2)}, u32[]{:S(2)}) %collective-permute-start.2) | collective-permute-done | bytes 262176 | tf_op jit(solution)/shard_map/while/body/eval_jaxpr/ppermute | solution.py:14
  181.5 0.9 constant_dynamic-slice_fusion.5
  184.2 8.9 %collective-permute-done.2 = f32[2,128,256]{1,2,0:T(8,128)S(1)} collective-permute-done((f32[2,128,256]{1,2,0:T(8,128)S(1)}, f32[2,128,256]{1,2,0:T(8,128)S(1)}, u32[]{:S(2)}, u32[]{:S(2)}) %collective-permute-start.2) | collective-permute-done | bytes 262176 | tf_op jit(solution)/shard_map/while/body/eval_jaxpr/ppermute | solution.py:14
  195.0 0.9 constant_dynamic-slice_fusion.5
  197.7 8.7 %collective-permute-done.2 = f32[2,128,256]{1,2,0:T(8,128)S(1)} collective-permute-done((f32[2,128,256]{1,2,0:T(8,128)S(1)}, f32[2,128,256]{1,2,0:T(8,128)S(1)}, u32[]{:S(2)}, u32[]{:S(2)}) %collective-permute-start.2) | collective-permute-done | bytes 262176 | tf_op jit(solution)/shard_map/while/body/eval_jaxpr/ppermute | solution.py:14
  206.4 1.3 fusion.27
  207.8 1.0 copy.123
  208.9 0.8 copy-done.5
  (191 shorter events, 35.2 us)
Async XLA Ops:
  0.6 5.6 %copy-start.7 = (bf16[128,2048]{1,0:T(8,128)(2,1)S(1)}, bf16[128,2048]{1,0:T(8,128)(2,1)}, u32[]{:S(2)}) copy-start(bf16[128,2048]{1,0:T(8,128)(2,1)} %param.12) | copy-start | bytes 1572868
  2.8 6.2 %copy-start.10 = (pred[128,128]{0,1:T(8,128)(4,1)}, pred[128,128]{0,1:T(8,128)(4,1)S(1)}, u32[]{:S(2)}) copy-start(pred[128,128]{0,1:T(8,128)(4,1)S(1)} %iota_compare_fusion) | copy-start | bytes 49156
  3.8 0.7 copy-start.3
  6.5 0.8 slice-start
  7.7 0.9 copy-start.4
  9.5 11.6 %collective-permute-start = (bf16[2,128,256]{1,2,0:T(8,128)(2,1)S(1)}, bf16[2,128,256]{1,2,0:T(8,128)(2,1)S(1)}, u32[]{:S(2)}, u32[]{:S(2)}) collective-permute-start(bf16[2,128,256]{1,2,0:T(8,128)(2,1)S(1)} %get-tuple-element.805), channel_id=1, source_target_pairs={{0,2},{2,4},{4,6},{6,8},{8,10},{10,12},{12,14},{14,0},{1,3},{3,5},... | collective-permute-start | bytes 393224 | tf_op jit(solution)/shard_map/while/body/eval_jaxpr/ppermute | solution.py:14
  12.5 6.7 %collective-permute-start.1 = (s32[1]{0:T(128)}, s32[1]{0:T(128)}, u32[]{:S(2)}, u32[]{:S(2)}) collective-permute-start(s32[1]{0:T(128)} %copy.192), channel_id=1, source_target_pairs={{0,2},{2,4},{4,6},{6,8},{8,10},{10,12},{12,14},{14,0},{1,3},{3,5},... | collective-permute-start | bytes 20 | tf_op jit(solution)/shard_map/while/body/eval_jaxpr/ppermute | solution.py:14
  22.3 9.8 %collective-permute-start = (bf16[2,128,256]{1,2,0:T(8,128)(2,1)S(1)}, bf16[2,128,256]{1,2,0:T(8,128)(2,1)S(1)}, u32[]{:S(2)}, u32[]{:S(2)}) collective-permute-start(bf16[2,128,256]{1,2,0:T(8,128)(2,1)S(1)} %get-tuple-element.805), channel_id=1, source_target_pairs={{0,2},{2,4},{4,6},{6,8},{8,10},{10,12},{12,14},{14,0},{1,3},{3,5},... | collective-permute-start | bytes 393224 | tf_op jit(solution)/shard_map/while/body/eval_jaxpr/ppermute | solution.py:14
  22.4 7.8 %collective-permute-start.1 = (s32[1]{0:T(128)}, s32[1]{0:T(128)}, u32[]{:S(2)}, u32[]{:S(2)}) collective-permute-start(s32[1]{0:T(128)} %copy.192), channel_id=1, source_target_pairs={{0,2},{2,4},{4,6},{6,8},{8,10},{10,12},{12,14},{14,0},{1,3},{3,5},... | collective-permute-start | bytes 20 | tf_op jit(solution)/shard_map/while/body/eval_jaxpr/ppermute | solution.py:14
  33.3 9.8 %collective-permute-start = (bf16[2,128,256]{1,2,0:T(8,128)(2,1)S(1)}, bf16[2,128,256]{1,2,0:T(8,128)(2,1)S(1)}, u32[]{:S(2)}, u32[]{:S(2)}) collective-permute-start(bf16[2,128,256]{1,2,0:T(8,128)(2,1)S(1)} %get-tuple-element.805), channel_id=1, source_target_pairs={{0,2},{2,4},{4,6},{6,8},{8,10},{10,12},{12,14},{14,0},{1,3},{3,5},... | collective-permute-start | bytes 393224 | tf_op jit(solution)/shard_map/while/body/eval_jaxpr/ppermute | solution.py:14
  33.4 7.8 %collective-permute-start.1 = (s32[1]{0:T(128)}, s32[1]{0:T(128)}, u32[]{:S(2)}, u32[]{:S(2)}) collective-permute-start(s32[1]{0:T(128)} %copy.192), channel_id=1, source_target_pairs={{0,2},{2,4},{4,6},{6,8},{8,10},{10,12},{12,14},{14,0},{1,3},{3,5},... | collective-permute-start | bytes 20 | tf_op jit(solution)/shard_map/while/body/eval_jaxpr/ppermute | solution.py:14
  44.4 9.8 %collective-permute-start = (bf16[2,128,256]{1,2,0:T(8,128)(2,1)S(1)}, bf16[2,128,256]{1,2,0:T(8,128)(2,1)S(1)}, u32[]{:S(2)}, u32[]{:S(2)}) collective-permute-start(bf16[2,128,256]{1,2,0:T(8,128)(2,1)S(1)} %get-tuple-element.805), channel_id=1, source_target_pairs={{0,2},{2,4},{4,6},{6,8},{8,10},{10,12},{12,14},{14,0},{1,3},{3,5},... | collective-permute-start | bytes 393224 | tf_op jit(solution)/shard_map/while/body/eval_jaxpr/ppermute | solution.py:14
  44.4 7.8 %collective-permute-start.1 = (s32[1]{0:T(128)}, s32[1]{0:T(128)}, u32[]{:S(2)}, u32[]{:S(2)}) collective-permute-start(s32[1]{0:T(128)} %copy.192), channel_id=1, source_target_pairs={{0,2},{2,4},{4,6},{6,8},{8,10},{10,12},{12,14},{14,0},{1,3},{3,5},... | collective-permute-start | bytes 20 | tf_op jit(solution)/shard_map/while/body/eval_jaxpr/ppermute | solution.py:14
  55.4 9.8 %collective-permute-start = (bf16[2,128,256]{1,2,0:T(8,128)(2,1)S(1)}, bf16[2,128,256]{1,2,0:T(8,128)(2,1)S(1)}, u32[]{:S(2)}, u32[]{:S(2)}) collective-permute-start(bf16[2,128,256]{1,2,0:T(8,128)(2,1)S(1)} %get-tuple-element.805), channel_id=1, source_target_pairs={{0,2},{2,4},{4,6},{6,8},{8,10},{10,12},{12,14},{14,0},{1,3},{3,5},... | collective-permute-start | bytes 393224 | tf_op jit(solution)/shard_map/while/body/eval_jaxpr/ppermute | solution.py:14
  55.5 7.8 %collective-permute-start.1 = (s32[1]{0:T(128)}, s32[1]{0:T(128)}, u32[]{:S(2)}, u32[]{:S(2)}) collective-permute-start(s32[1]{0:T(128)} %copy.192), channel_id=1, source_target_pairs={{0,2},{2,4},{4,6},{6,8},{8,10},{10,12},{12,14},{14,0},{1,3},{3,5},... | collective-permute-start | bytes 20 | tf_op jit(solution)/shard_map/while/body/eval_jaxpr/ppermute | solution.py:14
  66.4 9.8 %collective-permute-start = (bf16[2,128,256]{1,2,0:T(8,128)(2,1)S(1)}, bf16[2,128,256]{1,2,0:T(8,128)(2,1)S(1)}, u32[]{:S(2)}, u32[]{:S(2)}) collective-permute-start(bf16[2,128,256]{1,2,0:T(8,128)(2,1)S(1)} %get-tuple-element.805), channel_id=1, source_target_pairs={{0,2},{2,4},{4,6},{6,8},{8,10},{10,12},{12,14},{14,0},{1,3},{3,5},... | collective-permute-start | bytes 393224 | tf_op jit(solution)/shard_map/while/body/eval_jaxpr/ppermute | solution.py:14
  66.5 7.8 %collective-permute-start.1 = (s32[1]{0:T(128)}, s32[1]{0:T(128)}, u32[]{:S(2)}, u32[]{:S(2)}) collective-permute-start(s32[1]{0:T(128)} %copy.192), channel_id=1, source_target_pairs={{0,2},{2,4},{4,6},{6,8},{8,10},{10,12},{12,14},{14,0},{1,3},{3,5},... | collective-permute-start | bytes 20 | tf_op jit(solution)/shard_map/while/body/eval_jaxpr/ppermute | solution.py:14
  77.5 9.8 %collective-permute-start = (bf16[2,128,256]{1,2,0:T(8,128)(2,1)S(1)}, bf16[2,128,256]{1,2,0:T(8,128)(2,1)S(1)}, u32[]{:S(2)}, u32[]{:S(2)}) collective-permute-start(bf16[2,128,256]{1,2,0:T(8,128)(2,1)S(1)} %get-tuple-element.805), channel_id=1, source_target_pairs={{0,2},{2,4},{4,6},{6,8},{8,10},{10,12},{12,14},{14,0},{1,3},{3,5},... | collective-permute-start | bytes 393224 | tf_op jit(solution)/shard_map/while/body/eval_jaxpr/ppermute | solution.py:14
  77.5 7.8 %collective-permute-start.1 = (s32[1]{0:T(128)}, s32[1]{0:T(128)}, u32[]{:S(2)}, u32[]{:S(2)}) collective-permute-start(s32[1]{0:T(128)} %copy.192), channel_id=1, source_target_pairs={{0,2},{2,4},{4,6},{6,8},{8,10},{10,12},{12,14},{14,0},{1,3},{3,5},... | collective-permute-start | bytes 20 | tf_op jit(solution)/shard_map/while/body/eval_jaxpr/ppermute | solution.py:14
  88.5 0.5 copy-start.13
  88.5 1.8 copy-start.1
  90.3 1.0 copy-start.8
  90.3 1.2 copy-start.9
  95.4 1.4 copy-start.11
  96.8 1.0 copy-start.12
  102.7 1.1 copy-start
  103.6 1.1 copy-start.2
  105.3 0.6 copy-start.14
  110.1 9.4 %collective-permute-start.2 = (f32[2,128,256]{1,2,0:T(8,128)S(1)}, f32[2,128,256]{1,2,0:T(8,128)S(1)}, u32[]{:S(2)}, u32[]{:S(2)}) collective-permute-start(f32[2,128,256]{1,2,0:T(8,128)S(1)} %maximum_add_fusion.3), channel_id=1, source_target_pairs={{0,2},{2,4},{4,6},{6,8},{8,10},{10,12},{12,14},{14,0},{1,3},{3,5},... | collective-permute-start | bytes 786440 | tf_op jit(solution)/shard_map/while/body/eval_jaxpr/ppermute | solution.py:14
  123.7 10.5 %collective-permute-start.2 = (f32[2,128,256]{1,2,0:T(8,128)S(1)}, f32[2,128,256]{1,2,0:T(8,128)S(1)}, u32[]{:S(2)}, u32[]{:S(2)}) collective-permute-start(f32[2,128,256]{1,2,0:T(8,128)S(1)} %maximum_add_fusion.3), channel_id=1, source_target_pairs={{0,2},{2,4},{4,6},{6,8},{8,10},{10,12},{12,14},{14,0},{1,3},{3,5},... | collective-permute-start | bytes 786440 | tf_op jit(solution)/shard_map/while/body/eval_jaxpr/ppermute | solution.py:14
  138.3 11.6 %collective-permute-start.2 = (f32[2,128,256]{1,2,0:T(8,128)S(1)}, f32[2,128,256]{1,2,0:T(8,128)S(1)}, u32[]{:S(2)}, u32[]{:S(2)}) collective-permute-start(f32[2,128,256]{1,2,0:T(8,128)S(1)} %maximum_add_fusion.3), channel_id=1, source_target_pairs={{0,2},{2,4},{4,6},{6,8},{8,10},{10,12},{12,14},{14,0},{1,3},{3,5},... | collective-permute-start | bytes 786440 | tf_op jit(solution)/shard_map/while/body/eval_jaxpr/ppermute | solution.py:14
  154.1 11.1 %collective-permute-start.2 = (f32[2,128,256]{1,2,0:T(8,128)S(1)}, f32[2,128,256]{1,2,0:T(8,128)S(1)}, u32[]{:S(2)}, u32[]{:S(2)}) collective-permute-start(f32[2,128,256]{1,2,0:T(8,128)S(1)} %maximum_add_fusion.3), channel_id=1, source_target_pairs={{0,2},{2,4},{4,6},{6,8},{8,10},{10,12},{12,14},{14,0},{1,3},{3,5},... | collective-permute-start | bytes 786440 | tf_op jit(solution)/shard_map/while/body/eval_jaxpr/ppermute | solution.py:14
  169.4 10.3 %collective-permute-start.2 = (f32[2,128,256]{1,2,0:T(8,128)S(1)}, f32[2,128,256]{1,2,0:T(8,128)S(1)}, u32[]{:S(2)}, u32[]{:S(2)}) collective-permute-start(f32[2,128,256]{1,2,0:T(8,128)S(1)} %maximum_add_fusion.3), channel_id=1, source_target_pairs={{0,2},{2,4},{4,6},{6,8},{8,10},{10,12},{12,14},{14,0},{1,3},{3,5},... | collective-permute-start | bytes 786440 | tf_op jit(solution)/shard_map/while/body/eval_jaxpr/ppermute | solution.py:14
  183.8 9.3 %collective-permute-start.2 = (f32[2,128,256]{1,2,0:T(8,128)S(1)}, f32[2,128,256]{1,2,0:T(8,128)S(1)}, u32[]{:S(2)}, u32[]{:S(2)}) collective-permute-start(f32[2,128,256]{1,2,0:T(8,128)S(1)} %maximum_add_fusion.3), channel_id=1, source_target_pairs={{0,2},{2,4},{4,6},{6,8},{8,10},{10,12},{12,14},{14,0},{1,3},{3,5},... | collective-permute-start | bytes 786440 | tf_op jit(solution)/shard_map/while/body/eval_jaxpr/ppermute | solution.py:14
  197.3 9.1 %collective-permute-start.2 = (f32[2,128,256]{1,2,0:T(8,128)S(1)}, f32[2,128,256]{1,2,0:T(8,128)S(1)}, u32[]{:S(2)}, u32[]{:S(2)}) collective-permute-start(f32[2,128,256]{1,2,0:T(8,128)S(1)} %maximum_add_fusion.3), channel_id=1, source_target_pairs={{0,2},{2,4},{4,6},{6,8},{8,10},{10,12},{12,14},{14,0},{1,3},{3,5},... | collective-permute-start | bytes 786440 | tf_op jit(solution)/shard_map/while/body/eval_jaxpr/ppermute | solution.py:14
  208.8 0.9 copy-start.5
  208.8 1.0 copy-start.6
where the time goes:
time: 212 us; the launch traced here: 210 us
  waiting for transfers between devices  104 us (49%)
  local copies, waits for them, and re-layouts  30.8 us (15%)
  loops' own time  22.6 us (11%)
  starting transfers between devices  21.9 us (10%)
  matrix products  21.4 us (10%)
  other arithmetic  6.11 us (3%)
  between operations  3.65 us (2%)
    ppermute x21, waiting for transfers between devices, passed_along(): lax.ppermute(array, axis, [(i, (i + by) % count) for i in range(count)])  104 us
    ppermute x21, starting transfers between devices, passed_along(): lax.ppermute(array, axis, [(i, (i + by) % count) for i in range(count)])  21.9 us
    another operation x1, loops' own time, on_device(): lax.fori_loop(1, group_size, forward_turn, (prompt_kv, block_position, st...  13 us
    another operation x1, loops' own time, on_device(): lax.fori_loop(0, group_size - 1, backward_turn, (empty_block, query_grad))  9.51 us
    unnamed x35, local copies, waits for them, and re-layouts  7.33 us
    dot_general x17, matrix products, logits(): jnp.einsum('rgjd,tgd->gjrt', queries, key_rows, preferred_element_type=jn...  6.45 us
    slice x8, local copies, waits for them, and re-layouts, backward_part(): value_rows = kv_block[1].reshape(-1, kv_heads, HD)  6.25 us
    dynamic_update_slice x7, local copies, waits for them, and re-layouts, forward_turn(): lax.dynamic_update_index_in_dim(stash_pos, position[0], source, 0)  4.74 us
  transfers between devices with their start and end apart: 21, of which 14 were waited for; matrix products, arithmetic and copies ran while one was open for 3% of the time, Pallas kernels for 0%

commit v1 on v0

v1 whole, which is shorter than its diff:
```python
import functools
import math

import jax
import jax.numpy as jnp
from jax import lax
from jax.experimental import pallas as pl
from jax.experimental.pallas import tpu as pltpu
from jax.sharding import PartitionSpec as P

HD = 128
POS_ROWS = 16
COLS = 256
BLOCKED = -1e30
NT = (((1,), (1,)), ((), ()))


def dot(a, b):
    return jnp.dot(a, b, preferred_element_type=jnp.float32)


def dot_nt(a, b):
    return lax.dot_general(a, b, NT, preferred_element_type=jnp.float32)


def kernel(
    n, stride, kv_heads, ratio, rows,
    q_hbm, o_hbm, do_hbm, rkv_hbm, pkv_hbm, prefix_ref, len_ref, pos_ref,
    dq_ref, drkv_ref, dpkv_ref,
    q_in, o_in, do_in, q_all, do_all, kbuf, vbuf, k_t, delta, top, total,
    st, pb, ds, part, snd, rcv,
    in_sem, kv_sem, ag_send, ag_recv, rs_send, rs_recv,
):
    half = n // 2
    wide = ratio * rows
    chunks = wide // COLS
    scale = HD ** (-0.5)
    fold = scale * math.log2(math.e)

    order = {half: 2 * half}
    for step in range(2, half + 1):
        order[half + step - 1] = 2 * (step - 2)
        order[half - step + 1] = 2 * (step - 2) + 1
    order[0] = 2 * (half - 1)
    order[n] = 2 * (half - 1) + 1

    index = lax.axis_index("resp")
    me = index // stride
    lane = index % stride
    if stride == 1:
        x = me % 2
        z = me // 2
        last = (z + 1) // half
        first = (half - z) // half
        right = me + (1 - x) * (2 - last) + x * (first - 2)
        left = me + (1 - x) * (3 * first - 2) + x * (2 - 3 * last)
    else:
        right = (me + 1) % n
        left = (me + n - 1) % n
    right = right * stride + lane
    left = left * stride + lane

    kv_copies = []
    for g in range(kv_heads):
        cols = pl.ds(g * HD, HD)
        kv_copies.append(pltpu.make_async_copy(
            pkv_hbm.at[0, :, cols], kbuf.at[g, order[0], pl.ds(0, rows)], kv_sem.at[0, g]))
        kv_copies.append(pltpu.make_async_copy(
            pkv_hbm.at[1, :, cols], vbuf.at[g, order[0]], kv_sem.at[1, g]))
        kv_copies.append(pltpu.make_async_copy(
            rkv_hbm.at[0, :, cols], kbuf.at[g, order[n], pl.ds(0, rows)], kv_sem.at[2, g]))
        kv_copies.append(pltpu.make_async_copy(
            rkv_hbm.at[1, :, cols], vbuf.at[g, order[n]], kv_sem.at[3, g]))
    in_copies = [
        pltpu.make_async_copy(q_hbm, q_in, in_sem.at[0]),
        pltpu.make_async_copy(do_hbm, do_in, in_sem.at[1]),
        pltpu.make_async_copy(o_hbm, o_in, in_sem.at[2]),
    ]
    for copy in kv_copies + in_copies:
        copy.start()

    barrier = pltpu.get_barrier_semaphore()
    for near in (left, right):
        pl.semaphore_signal(
            barrier, inc=1, device_id={"resp": near}, device_id_type=pl.DeviceIdType.MESH)
    position = jnp.full((POS_ROWS, HD), pos_ref[0], jnp.int32).astype(jnp.float32)
    for g in range(kv_heads):
        kbuf[g, order[0], rows:rows + POS_ROWS, :] = position.astype(jnp.bfloat16)
    pl.semaphore_wait(barrier, 2)
    for copy in kv_copies:
        copy.wait()

    def send(src, dst, send_sem, recv_sem, way):
        return pltpu.make_async_remote_copy(
            src_ref=src, dst_ref=dst, send_sem=send_sem, recv_sem=recv_sem,
            device_id={"resp": right if way == 0 else left},
            device_id_type=pl.DeviceIdType.MESH)

    def gather_copy(kind, way, step):
        buf = kbuf if kind == 0 else vbuf
        if way == 0:
            source, target = order[step - 1], order[step]
        else:
            source, target = order[(n - step + 1) % n], order[n - step]
        if step == half:
            src, dst = buf.at[way, source], buf.at[way, target]
        else:
            src, dst = buf.at[:, source], buf.at[:, target]
        return send(src, dst, ag_send.at[kind, way, step - 1], ag_recv.at[kind, way, step - 1], way)

    gather = {
        (kind, way, step): gather_copy(kind, way, step)
        for kind in range(2) for way in range(2) for step in range(1, half + 1)
    }

    def start_gather(kind, step):
        for way in range(2):
            gather[kind, way, step].start()

    def wait_gather(kind, step):
        for way in range(2):
            gather[kind, way, step].wait_recv()

    start_gather(0, 1)
    start_gather(1, 1)

    for copy in in_copies:
        copy.wait()
    live = lax.broadcasted_iota(jnp.int32, (rows, HD), 0) < len_ref[0]
    for g in range(kv_heads):
        for j in range(ratio):
            cols = slice((g * ratio + j) * HD, (g * ratio + j + 1) * HD)
            place = slice(j * rows, (j + 1) * rows)
            q_all[g, place, :] = q_in[:, cols]
            grads = jnp.where(live, do_in[:, cols].astype(jnp.float32), 0.0)
            do_all[g, place, :] = grads.astype(jnp.bfloat16)
            product = jnp.transpose(grads * o_in[:, cols].astype(jnp.float32))
            delta[g, :, place] = jnp.sum(product, axis=0, keepdims=True)

    def forward(slot, start=False):
        spot = order[slot]
        if slot == n:
            allowed = None
        else:
            seen = kbuf[0, spot, rows:rows + 8, :].astype(jnp.float32)[0:1, :]
            bias = jnp.where(seen < prefix_ref[0].astype(jnp.float32), 0.0, BLOCKED)
            bias = jnp.concatenate([bias] * (COLS // HD), axis=1)

        def head(g, carry):
            keys = kbuf[g, spot, 0:rows, :]
            k_t[g, :, spot * rows:(spot + 1) * rows] = jnp.transpose(
                keys.astype(jnp.float32)).astype(jnp.bfloat16)
            for c in range(chunks):
                cols = slice(c * COLS, (c + 1) * COLS)
                scores = dot_nt(keys, q_all[g, cols, :]) * fold
                if slot == n:
                    key_index = lax.broadcasted_iota(jnp.int32, (rows, COLS), 0)
                    row_index = lax.broadcasted_iota(jnp.int32, (rows, COLS), 1) % rows
                    scores = jnp.where(key_index <= row_index, scores, BLOCKED)
                else:
                    scores = scores + bias
                st[g, spot * rows:(spot + 1) * rows, cols] = scores
                peak = jnp.max(scores, axis=0, keepdims=True)
                if start:
                    top[g, :, cols] = peak
                    total[g, :, cols] = jnp.sum(jnp.exp2(scores - peak), axis=0, keepdims=True)
                else:
                    old = top[g, :, cols]
                    new = jnp.maximum(old, peak)
                    top[g, :, cols] = new
                    total[g, :, cols] = total[g, :, cols] * jnp.exp2(old - new) + jnp.sum(
                        jnp.exp2(scores - new), axis=0, keepdims=True)
            return carry

        lax.fori_loop(0, kv_heads, head, 0)

    forward(n, True)
    forward(0)
    for step in range(1, half + 1):
        wait_gather(0, step)
        if step < half:
            start_gather(0, step + 1)
        if step > 1:
            wait_gather(1, step - 1)
            start_gather(1, step)
        forward(step)
        if step < half:
            forward(n - step)

    for g in range(kv_heads):
        top[g] = top[g] + jnp.log2(total[g])

    def value_side(spot, count):
        def head(g, carry):
            for b in range(count):
                span = slice((spot + b) * rows, (spot + b + 1) * rows)
                for c in range(chunks):
                    cols = slice(c * COLS, (c + 1) * COLS)
                    weights = jnp.exp2(st[g, span, cols] - top[g, :, cols])
                    st[g, span, cols] = weights
                    pb[b * rows:(b + 1) * rows, cols] = weights.astype(jnp.bfloat16)
            part[1, g, spot * rows:(spot + count) * rows, :] = dot(
                pb[0:count * rows, :], do_all[g])
            return carry

        lax.fori_loop(0, kv_heads, head, 0)

    def key_side(spot, count):
        def head(g, carry):
            for b in range(count):
                span = slice((spot + b) * rows, (spot + b + 1) * rows)
                values = vbuf[g, spot + b]
                for c in range(chunks):
                    cols = slice(c * COLS, (c + 1) * COLS)
                    moved = dot_nt(values, do_all[g, cols, :])
                    ds[g, span, cols] = (
                        st[g, span, cols] * (moved - delta[g, :, cols]) * scale
                    ).astype(jnp.bfloat16)
            part[0, g, spot * rows:(spot + count) * rows, :] = dot(
                ds[g, spot * rows:(spot + count) * rows, :], q_all[g])
            return carry

        lax.fori_loop(0, kv_heads, head, 0)

    def own(kind, g, spot):
        return part[kind, g, spot * rows:(spot + 1) * rows, :]

    def back_copy(kind, way, step):
        src, dst = snd.at[kind, way, step - 1], rcv.at[kind, way, step - 1]
        if step == 1:
            src, dst = src.at[way], dst.at[way]
        return send(src, dst, rs_send.at[kind, way, step - 1], rs_recv.at[kind, way, step - 1], way)

    back = {
        (kind, way, step): back_copy(kind, way, step)
        for kind in range(2) for way in range(2) for step in range(1, half + 1)
    }

    value_side(order[half], 1)
    for way in range(2):
        snd[1, way, 0, way] = own(1, way, order[half]).astype(jnp.bfloat16)
        back[1, way, 1].start()
    wait_gather(1, half)
    key_side(order[half], 1)
    for way in range(2):
        snd[0, way, 0, way] = own(0, way, order[half]).astype(jnp.bfloat16)
        back[0, way, 1].start()

    for step in range(2, half + 1):
        spot = 2 * (step - 2)
        value_side(spot, 2)
        key_side(spot, 2)
        for kind in (1, 0):
            for way in range(2):
                back[kind, way, step - 1].wait_recv()
                for g in range(kv_heads):
                    mine = own(kind, g, spot + way)
                    if step > 2 or g == way:
                        mine = mine + rcv[kind, way, step - 2, g].astype(jnp.float32)
                    snd[kind, way, step - 1, g] = mine.astype(jnp.bfloat16)
                back[kind, way, step].start()

    spot = 2 * (half - 1)
    value_side(spot, 2)
    key_side(spot, 2)
    for kind in range(2):
        for g in range(kv_heads):
            drkv_ref[kind, :, g * HD:(g + 1) * HD] = own(kind, g, spot + 1).astype(jnp.bfloat16)
    for g in range(kv_heads):
        for c in range(chunks):
            turned = dot(k_t[g], ds[g, :, c * COLS:(c + 1) * COLS])
            for j in range(COLS // rows):
                column = (g * ratio + c * (COLS // rows) + j) * HD
                dq_ref[:, column:column + HD] = jnp.transpose(
                    turned[:, j * rows:(j + 1) * rows]).astype(jnp.bfloat16)
    for kind in (1, 0):
        for way in range(2):
            back[kind, way, half].wait_recv()
        for g in range(kv_heads):
            summed = own(kind, g, spot)
            for way in range(2):
                summed = summed + rcv[kind, way, half - 1, g].astype(jnp.float32)
            dpkv_ref[kind, :, g * HD:(g + 1) * HD] = summed.astype(jnp.bfloat16)

    for copy in list(gather.values()) + list(back.values()):
        copy.wait_send()


def on_device(query, saved_out, d_out, resp_kv, prompt_kv, prefix_blocks, resp_len, block_position):
    rows = query.shape[0]
    kv_heads = resp_kv.shape[2] // HD
    ratio = query.shape[1] // HD // kv_heads
    axis_total = lax.axis_size("resp")
    n = min(16, axis_total)
    stride = axis_total // n
    half = n // 2
    wide = ratio * rows
    keys = (n + 1) * rows
    low, full = jnp.bfloat16, jnp.float32
    anywhere = pl.BlockSpec(memory_space=pl.ANY)
    vmem = pl.BlockSpec(memory_space=pltpu.VMEM)
    smem = pl.BlockSpec(memory_space=pltpu.SMEM)
    dma = pltpu.SemaphoreType.DMA
    return pl.pallas_call(
        functools.partial(kernel, n, stride, kv_heads, ratio, rows),
        out_shape=(
            jax.ShapeDtypeStruct(query.shape, low),
            jax.ShapeDtypeStruct(resp_kv.shape, low),
            jax.ShapeDtypeStruct(prompt_kv.shape, low),
        ),
        in_specs=[anywhere] * 5 + [smem] * 3,
        out_specs=(vmem, vmem, vmem),
        scratch_shapes=[
            pltpu.VMEM(query.shape, low),
            pltpu.VMEM(query.shape, low),
            pltpu.VMEM(query.shape, low),
            pltpu.VMEM((kv_heads, wide, HD), low),
            pltpu.VMEM((kv_heads, wide, HD), low),
            pltpu.VMEM((kv_heads, n + 1, rows + POS_ROWS, HD), low),
            pltpu.VMEM((kv_heads, n + 1, rows, HD), low),
            pltpu.VMEM((kv_heads, HD, keys), low),
            pltpu.VMEM((kv_heads, 1, wide), full),
            pltpu.VMEM((kv_heads, 1, wide), full),
            pltpu.VMEM((kv_heads, 1, wide), full),
            pltpu.VMEM((kv_heads, keys, wide), full),
            pltpu.VMEM((2 * rows, wide), low),
            pltpu.VMEM((kv_heads, keys, wide), low),
            pltpu.VMEM((2, kv_heads, keys, HD), full),
            pltpu.VMEM((2, 2, half, kv_heads, rows, HD), low),
            pltpu.VMEM((2, 2, half, kv_heads, rows, HD), low),
            dma((3,)),
            dma((4, kv_heads)),
            dma((2, 2, half)),
            dma((2, 2, half)),
            dma((2, 2, half)),
            dma((2, 2, half)),
        ],
        compiler_params=pltpu.CompilerParams(
            collective_id=0, has_side_effects=True, vmem_limit_bytes=56 * 2**20),
    )(query, saved_out, d_out, resp_kv, prompt_kv, prefix_blocks, resp_len, block_position)


def solution(mesh):
    placed = (
        P(("groups", "resp"), "mp"),
        P(("groups", "resp"), "mp"),
        P(("groups", "resp"), "mp"),
        P(None, ("groups", "resp"), "mp"),
        P(None, ("groups", "resp"), "mp"),
        P(("groups", "resp")),
        P(("groups", "resp")),
        P(("groups", "resp")),
    )
    return jax.shard_map(
        on_device,
        mesh=mesh,
        in_specs=placed,
        out_specs=(
            P(("groups", "resp"), "mp"),
            P(None, ("groups", "resp"), "mp"),
            P(None, ("groups", "resp"), "mp"),
        ),
        check_vma=False,
    )
```

time: 212 us -> 46.1 us (0.22)
  waiting for transfers between devices: 104 us -> 0 us
  Pallas kernels: 0 us -> 39.8 us
  local copies, waits for them, and re-layouts: 30.8 us -> 3.53 us
  loops' own time: 22.6 us -> 0 us
  starting transfers between devices: 21.9 us -> 0 us
  matrix products: 21.4 us -> 0 us
  other arithmetic: 6.11 us -> 0 us
    ppermute x21 -> x0, waiting for transfers between devices: 104 us -> none  [passed_along(): lax.ppermute(array, axis, [(i, (i + by) % count) for i in range(count)])]
    pallas_call x0 -> x1, Pallas kernels: none -> 39.8 us  [on_device(): pl.pallas_call(functools.partial(kernel, n, stride, kv_heads, ratio, rows...]
    another operation x2 -> x0, loops' own time: 22.6 us -> none  [the longest x1 13 us: on_device(): lax.fori_loop(1, group_size, forward_turn, (prompt_kv, block_position, st...]
    ppermute x21 -> x0, starting transfers between devices: 21.9 us -> none  [passed_along(): lax.ppermute(array, axis, [(i, (i + by) % count) for i in range(count)])]
    dot_general x53 -> x0, matrix products: 21.4 us -> none  [the longest x17 6.45 us: logits(): jnp.einsum('rgjd,tgd->gjrt', queries, key_rows, preferred_element_type=jn...]
    slice x18 -> x0, local copies, waits for them, and re-layouts: 7.72 us -> none  [the longest x8 6.25 us: backward_part(): value_rows = kv_block[1].reshape(-1, kv_heads, HD)]
    dynamic_update_slice x16 -> x0, local copies, waits for them, and re-layouts: 5.05 us -> none  [the longest x7 4.74 us: forward_turn(): lax.dynamic_update_index_in_dim(stash_pos, position[0], source, 0)]
    dynamic_slice x8 -> x0, local copies, waits for them, and re-layouts: 4.66 us -> none  [the longest x7 4.08 us: backward_turn(): part_query, part_block = back_block(stash[source], stash_pos[source])]
  transfers between devices with their start and end apart: 21 -> 0, of which waited for: 14 -> 0; matrix products, arithmetic and copies ran while one was open for 3% -> 0% of each run, Pallas kernels for 0% -> 0%
where the time goes in v1:
time: 46.1 us; the launch traced here: 45.9 us
  Pallas kernels  39.8 us (86%)
  local copies, waits for them, and re-layouts  3.53 us (8%)
  between operations  2.59 us (6%)
    pallas_call x1, Pallas kernels, on_device(): pl.pallas_call(functools.partial(kernel, n, stride, kv_heads, ratio, rows...  39.8 us
    unnamed x7, local copies, waits for them, and re-layouts  3.53 us

profile of v1, /device:TPU:0, one launch (start us, length us, event | category | flops | bytes accessed | tf_op | source)
XLA Modules:
  0.0 45.9 jit_solution(16949916158140962623)
XLA Ops:
  2.6 39.8 %shard_map.103 = (bf16[128,2048]{1,0:T(8,128)(2,1)}, bf16[2,128,256]{2,1,0:T(8,128)(2,1)}, bf16[2,128,256]{2,1,0:T(8,128)(2,1)}) custom-call(bf16[128,2048]{1,0:T(8,128)(2,1)} %q_hbm.1, bf16[128,2048]{1,0:T(8,128)(2,1)} %o_hbm.1, bf16[128,2048]{1,0:T(8,128)(2,1)} %do_hbm.1, bf16[2,128,256]{2,1,0:T(8,128)(2,1)} %rkv_hbm.1, bf16[2,128,256]{2,1,0:T(8,128)(2,1)} %pkv_hbm.1, ...), custom_call_target="tpu_custom_call" | custom-call | tf_op jit(solution)/shard_map/pallas_call | solution.py:304
  42.4 0.0 copy-start.1
  42.4 1.9 %copy.17 = bf16[128,2048]{1,0:T(8,128)(2,1)} copy(bf16[128,2048]{1,0:T(8,128)(2,1)} %get-tuple-element.6) | data formatting | bytes 1048576
  44.3 0.0 copy-done.1
  44.3 0.0 copy-start
  44.3 0.7 %copy.18 = bf16[2,128,256]{2,1,0:T(8,128)(2,1)} copy(bf16[2,128,256]{2,1,0:T(8,128)(2,1)S(1)} %copy-done.1) | data formatting | bytes 262144
  44.9 0.3 copy-done
  45.2 0.7 %copy.19 = bf16[2,128,256]{2,1,0:T(8,128)(2,1)} copy(bf16[2,128,256]{2,1,0:T(8,128)(2,1)S(1)} %copy-done) | data formatting | bytes 262144
Async XLA Ops:
  42.4 1.9 %copy-start.1 = (bf16[2,128,256]{2,1,0:T(8,128)(2,1)S(1)}, bf16[2,128,256]{2,1,0:T(8,128)(2,1)}, u32[]{:S(2)}) copy-start(bf16[2,128,256]{2,1,0:T(8,128)(2,1)} %get-tuple-element.7) | copy-start | bytes 393220
  44.3 1.0 %copy-start = (bf16[2,128,256]{2,1,0:T(8,128)(2,1)S(1)}, bf16[2,128,256]{2,1,0:T(8,128)(2,1)}, u32[]{:S(2)}) copy-start(bf16[2,128,256]{2,1,0:T(8,128)(2,1)} %get-tuple-element.8) | copy-start | bytes 393220

commit v2 on v1

--- a/solution.py
+++ b/solution.py
@@ -28,8 +28,8 @@
     q_hbm, o_hbm, do_hbm, rkv_hbm, pkv_hbm, prefix_ref, len_ref, pos_ref,
     dq_ref, drkv_ref, dpkv_ref,
     q_in, o_in, do_in, q_all, do_all, kbuf, vbuf, k_t, delta, top, total,
-    st, pb, ds, part, snd, rcv,
-    in_sem, kv_sem, ag_send, ag_recv, rs_send, rs_recv,
+    st, pb, ds, part, snd, rcv, drkv, dpkv,
+    in_sem, out_sem, kv_sem, ag_send, ag_recv, rs_send, rs_recv,
 ):
     half = n // 2
     wide = ratio * rows
@@ -96,33 +96,35 @@
             device_id={"resp": right if way == 0 else left},
             device_id_type=pl.DeviceIdType.MESH)
 
-    def gather_copy(kind, way, step):
+    def gather_copy(kind, way, step, g):
         buf = kbuf if kind == 0 else vbuf
         if way == 0:
             source, target = order[step - 1], order[step]
         else:
             source, target = order[(n - step + 1) % n], order[n - step]
-        if step == half:
-            src, dst = buf.at[way, source], buf.at[way, target]
-        else:
-            src, dst = buf.at[:, source], buf.at[:, target]
-        return send(src, dst, ag_send.at[kind, way, step - 1], ag_recv.at[kind, way, step - 1], way)
+        return send(
+            buf.at[g, source], buf.at[g, target],
+            ag_send.at[kind, way, step - 1, g], ag_recv.at[kind, way, step - 1, g], way)
+
+    def carried(way, step, g):
+        return step < half or g == way
 
     gather = {
-        (kind, way, step): gather_copy(kind, way, step)
+        (kind, way, step, g): gather_copy(kind, way, step, g)
         for kind in range(2) for way in range(2) for step in range(1, half + 1)
+        for g in range(kv_heads) if carried(way, step, g)
     }
 
-    def start_gather(kind, step):
-        for way in range(2):
-            gather[kind, way, step].start()
-
-    def wait_gather(kind, step):
-        for way in range(2):
-            gather[kind, way, step].wait_recv()
-
-    start_gather(0, 1)
-    start_gather(1, 1)
+    def pass_on(kind, step):
+        for g in range(kv_heads):
+            for way in range(2):
+                if step > 0 and (kind, way, step, g) in gather:
+                    gather[kind, way, step, g].wait_recv()
+                if (kind, way, step + 1, g) in gather:
+                    gather[kind, way, step + 1, g].start()
+
+    pass_on(0, 0)
+    pass_on(1, 0)
 
     for copy in in_copies:
         copy.wait()
@@ -177,12 +179,9 @@
     forward(n, True)
     forward(0)
     for step in range(1, half + 1):
-        wait_gather(0, step)
+        pass_on(0, step)
         if step < half:
-            start_gather(0, step + 1)
-        if step > 1:
-            wait_gather(1, step - 1)
-            start_gather(1, step)
+            pass_on(1, step)
         forward(step)
         if step < half:
             forward(n - step)
@@ -225,65 +224,89 @@
     def own(kind, g, spot):
         return part[kind, g, spot * rows:(spot + 1) * rows, :]
 
-    def back_copy(kind, way, step):
-        src, dst = snd.at[kind, way, step - 1], rcv.at[kind, way, step - 1]
-        if step == 1:
-            src, dst = src.at[way], dst.at[way]
-        return send(src, dst, rs_send.at[kind, way, step - 1], rs_recv.at[kind, way, step - 1], way)
+    def back_copy(kind, way, step, g):
+        return send(
+            snd.at[kind, way, step - 1, g], rcv.at[kind, way, step - 1, g],
+            rs_send.at[kind, way, step - 1, g], rs_recv.at[kind, way, step - 1, g], way)
 
     back = {
-        (kind, way, step): back_copy(kind, way, step)
+        (kind, way, step, g): back_copy(kind, way, step, g)
         for kind in range(2) for way in range(2) for step in range(1, half + 1)
+        for g in range(kv_heads) if step > 1 or g == way
     }
 
     value_side(order[half], 1)
     for way in range(2):
         snd[1, way, 0, way] = own(1, way, order[half]).astype(jnp.bfloat16)
-        back[1, way, 1].start()
-    wait_gather(1, half)
+        back[1, way, 1, way].start()
+    pass_on(1, half)
     key_side(order[half], 1)
     for way in range(2):
         snd[0, way, 0, way] = own(0, way, order[half]).astype(jnp.bfloat16)
-        back[0, way, 1].start()
+        back[0, way, 1, way].start()
 
     for step in range(2, half + 1):
         spot = 2 * (step - 2)
         value_side(spot, 2)
         key_side(spot, 2)
         for kind in (1, 0):
-            for way in range(2):
-                back[kind, way, step - 1].wait_recv()
-                for g in range(kv_heads):
-                    mine = own(kind, g, spot + way)
-                    if step > 2 or g == way:
-                        mine = mine + rcv[kind, way, step - 2, g].astype(jnp.float32)
-                    snd[kind, way, step - 1, g] = mine.astype(jnp.bfloat16)
-                back[kind, way, step].start()
+            pairs = [(g, way) for g in range(kv_heads) for way in range(2)]
+            if step == 2:
+                pairs.sort(key=lambda pair: pair[0] == pair[1])
+            for g, way in pairs:
+                mine = own(kind, g, spot + way)
+                if (kind, way, step - 1, g) in back:
+                    back[kind, way, step - 1, g].wait_recv()
+                    mine = mine + rcv[kind, way, step - 2, g].astype(jnp.float32)
+                snd[kind, way, step - 1, g] = mine.astype(jnp.bfloat16)
+                back[kind, way, step, g].start()
 
     spot = 2 * (half - 1)
     value_side(spot, 2)
     key_side(spot, 2)
     for kind in range(2):
         for g in range(kv_heads):
-            drkv_ref[kind, :, g * HD:(g + 1) * HD] = own(kind, g, spot + 1).astype(jnp.bfloat16)
+            drkv[kind, :, g * HD:(g + 1) * HD] = own(kind, g, spot + 1).astype(jnp.bfloat16)
     for g in range(kv_heads):
         for c in range(chunks):
             turned = dot(k_t[g], ds[g, :, c * COLS:(c + 1) * COLS])
             for j in range(COLS // rows):
                 column = (g * ratio + c * (COLS // rows) + j) * HD
-                dq_ref[:, column:column + HD] = jnp.transpose(
+                q_in[:, column:column + HD] = jnp.transpose(
                     turned[:, j * rows:(j + 1) * rows]).astype(jnp.bfloat16)
+    out_copies = [
+        pltpu.make_async_copy(q_in, dq_ref, out_sem.at[0]),
+        pltpu.make_async_copy(drkv, drkv_ref, out_sem.at[1]),
+        pltpu.make_async_copy(dpkv, dpkv_ref, out_sem.at[2]),
+    ]
+    out_copies[0].start()
+    out_copies[1].start()
     for kind in (1, 0):
-        for way in range(2):
-            back[kind, way, half].wait_recv()
         for g in range(kv_heads):
             summed = own(kind, g, spot)
             for way in range(2):
+                back[kind, way, half, g].wait_recv()
                 summed = summed + rcv[kind, way, half - 1, g].astype(jnp.float32)
-            dpkv_ref[kind, :, g * HD:(g + 1) * HD] = summed.astype(jnp.bfloat16)
+            dpkv[kind, :, g * HD:(g + 1) * HD] = summed.astype(jnp.bfloat16)
+    out_copies[2].start()
 
     for copy in list(gather.values()) + list(back.values()):
         copy.wait_send()
+    for copy in out_copies:
+        copy.wait()
+
+
+def hand_out(a, b, c, a_out, b_out, c_out, a_held, b_held, c_held, in_sem, out_sem):
+    triples = ((a, a_held, a_out), (b, b_held, b_out), (c, c_held, c_out))
+    taken = [pltpu.make_async_copy(t[0], t[1], in_sem.at[i]) for i, t in enumerate(triples)]
+    given = [pltpu.make_async_copy(t[1], t[2], out_sem.at[i]) for i, t in enumerate(triples)]
+    for copy in taken:
+        copy.start()
+    for copy, after in zip(taken, given):
+        copy.wait()
+        after.start()
+    for copy in given:
+        copy.wait()
 
 
 def on_device(query, saved_out, d_out, resp_kv, prompt_kv, prefix_blocks, resp_len, block_position):
@@ -298,10 +321,9 @@
     keys = (n + 1) * rows
     low, full = jnp.bfloat16, jnp.float32
     anywhere = pl.BlockSpec(memory_space=pl.ANY)
-    vmem = pl.BlockSpec(memory_space=pltpu.VMEM)
     smem = pl.BlockSpec(memory_space=pltpu.SMEM)
     dma = pltpu.SemaphoreType.DMA
-    return pl.pallas_call(
+    results = pl.pallas_call(
         functools.partial(kernel, n, stride, kv_heads, ratio, rows),
         out_shape=(
             jax.ShapeDtypeStruct(query.shape, low),
@@ -309,7 +331,7 @@
             jax.ShapeDtypeStruct(prompt_kv.shape, low),
         ),
         in_specs=[anywhere] * 5 + [smem] * 3,
-        out_specs=(vmem, vmem, vmem),
+        out_specs=(anywhere, anywhere, anywhere),
         scratch_shapes=[
             pltpu.VMEM(query.shape, low),
             pltpu.VMEM(query.shape, low),
@@ -328,16 +350,26 @@
             pltpu.VMEM((2, kv_heads, keys, HD), full),
             pltpu.VMEM((2, 2, half, kv_heads, rows, HD), low),
             pltpu.VMEM((2, 2, half, kv_heads, rows, HD), low),
+            pltpu.VMEM(resp_kv.shape, low),
+            pltpu.VMEM(prompt_kv.shape, low),
+            dma((3,)),
             dma((3,)),
             dma((4, kv_heads)),
-            dma((2, 2, half)),
-            dma((2, 2, half)),
-            dma((2, 2, half)),
-            dma((2, 2, half)),
+            dma((2, 2, half, kv_heads)),
+            dma((2, 2, half, kv_heads)),
+            dma((2, 2, half, kv_heads)),
+            dma((2, 2, half, kv_heads)),
         ],
         compiler_params=pltpu.CompilerParams(
             collective_id=0, has_side_effects=True, vmem_limit_bytes=56 * 2**20),
     )(query, saved_out, d_out, resp_kv, prompt_kv, prefix_blocks, resp_len, block_position)
+    return pl.pallas_call(
+        hand_out,
+        out_shape=tuple(jax.ShapeDtypeStruct(r.shape, r.dtype) for r in results),
+        in_specs=[anywhere] * 3,
+        out_specs=(anywhere,) * 3,
+        scratch_shapes=[pltpu.VMEM(r.shape, r.dtype) for r in results] + [dma((3,)), dma((3,))],
+    )(*results)
 
 
 def solution(mesh):

time: 46.1 us -> 40 us (0.87)
  local copies, waits for them, and re-layouts: 3.53 us -> 0 us
  Pallas kernels: 39.8 us -> 37.2 us
    pallas_call x1, Pallas kernels: 39.8 us -> 35.3 us  [on_device(): pl.pallas_call(functools.partial(kernel, n, stride, kv_heads, ratio, rows...]
    unnamed x7 -> x0, local copies, waits for them, and re-layouts: 3.53 us -> none
    pallas_call x0 -> x1, Pallas kernels: none -> 1.96 us  [on_device(): pl.pallas_call(hand_out, out_shape=tuple((jax.ShapeDtypeStruct(r.shape, r...]
where the time goes in v2:
time: 40 us; the launch traced here: 39.8 us
  Pallas kernels  37.2 us (93%)
  between operations  2.58 us (6%)
    pallas_call x1, Pallas kernels, on_device(): pl.pallas_call(functools.partial(kernel, n, stride, kv_heads, ratio, rows...  35.3 us
    pallas_call x1, Pallas kernels, on_device(): pl.pallas_call(hand_out, out_shape=tuple((jax.ShapeDtypeStruct(r.shape, r...  1.96 us

profile of v2, /device:TPU:0, one launch (start us, length us, event | category | flops | bytes accessed | tf_op | source)
XLA Modules:
  0.0 39.8 jit_solution(15253757747838277088)
XLA Ops:
  2.6 35.3 %shard_map.103 = (bf16[128,2048]{1,0:T(8,128)(2,1)}, bf16[2,128,256]{2,1,0:T(8,128)(2,1)}, bf16[2,128,256]{2,1,0:T(8,128)(2,1)}) custom-call(bf16[128,2048]{1,0:T(8,128)(2,1)} %q_hbm.1, bf16[128,2048]{1,0:T(8,128)(2,1)} %o_hbm.1, bf16[128,2048]{1,0:T(8,128)(2,1)} %do_hbm.1, bf16[2,128,256]{2,1,0:T(8,128)(2,1)} %rkv_hbm.1, bf16[2,128,256]{2,1,0:T(8,128)(2,1)} %pkv_hbm.1, ...), custom_call_target="tpu_custom_call" | custom-call | tf_op jit(solution)/shard_map/pallas_call | solution.py:326
  37.9 2.0 %shard_map.104 = (bf16[128,2048]{1,0:T(8,128)(2,1)}, bf16[2,128,256]{2,1,0:T(8,128)(2,1)}, bf16[2,128,256]{2,1,0:T(8,128)(2,1)}) custom-call(bf16[128,2048]{1,0:T(8,128)(2,1)} %get-tuple-element.6.a, bf16[2,128,256]{2,1,0:T(8,128)(2,1)} %get-tuple-element.7.b, bf16[2,128,256]{2,1,0:T(8,128)(2,1)} %get-tuple-element.8.c), custom_call_target="tpu_custom_call" | custom-call | tf_op jit(solution)/shard_map/pallas_call | solution.py:366

commit v3 on v2

--- a/solution.py
+++ b/solution.py
@@ -87,8 +87,9 @@
     for g in range(kv_heads):
         kbuf[g, order[0], rows:rows + POS_ROWS, :] = position.astype(jnp.bfloat16)
     pl.semaphore_wait(barrier, 2)
-    for copy in kv_copies:
-        copy.wait()
+    for g in range(kv_heads):
+        kv_copies[4 * g].wait()
+        kv_copies[4 * g + 1].wait()
 
     def send(src, dst, send_sem, recv_sem, way):
         return pltpu.make_async_remote_copy(
@@ -126,6 +127,9 @@
     pass_on(0, 0)
     pass_on(1, 0)
 
+    for g in range(kv_heads):
+        kv_copies[4 * g + 2].wait()
+        kv_copies[4 * g + 3].wait()
     for copy in in_copies:
         copy.wait()
     live = lax.broadcasted_iota(jnp.int32, (rows, HD), 0) < len_ref[0]
@@ -247,9 +251,11 @@
 
     for step in range(2, half + 1):
         spot = 2 * (step - 2)
-        value_side(spot, 2)
-        key_side(spot, 2)
         for kind in (1, 0):
+            if kind == 1:
+                value_side(spot, 2)
+            else:
+                key_side(spot, 2)
             pairs = [(g, way) for g in range(kv_heads) for way in range(2)]
             if step == 2:
                 pairs.sort(key=lambda pair: pair[0] == pair[1])
@@ -297,7 +303,11 @@
 
 
 def hand_out(a, b, c, a_out, b_out, c_out, a_held, b_held, c_held, in_sem, out_sem):
-    triples = ((a, a_held, a_out), (b, b_held, b_out), (c, c_held, c_out))
+    triples = [(b, b_held, b_out), (c, c_held, c_out)]
+    quarter = a.shape[0] // 4
+    for i in range(4):
+        span = pl.ds(i * quarter, quarter)
+        triples.append((a.at[span], a_held.at[span], a_out.at[span]))
     taken = [pltpu.make_async_copy(t[0], t[1], in_sem.at[i]) for i, t in enumerate(triples)]
     given = [pltpu.make_async_copy(t[1], t[2], out_sem.at[i]) for i, t in enumerate(triples)]
     for copy in taken:
@@ -368,7 +378,7 @@
         out_shape=tuple(jax.ShapeDtypeStruct(r.shape, r.dtype) for r in results),
         in_specs=[anywhere] * 3,
         out_specs=(anywhere,) * 3,
-        scratch_shapes=[pltpu.VMEM(r.shape, r.dtype) for r in results] + [dma((3,)), dma((3,))],
+        scratch_shapes=[pltpu.VMEM(r.shape, r.dtype) for r in results] + [dma((6,)), dma((6,))],
     )(*results)
 
 

time: 40 us -> 40 us (level)
  no operation moved by 1% of the time
where the time goes in v3:
time: 40 us; the launch traced here: 39.8 us
  Pallas kernels  37.2 us (93%)
  between operations  2.58 us (6%)
    pallas_call x1, Pallas kernels, on_device(): pl.pallas_call(functools.partial(kernel, n, stride, kv_heads, ratio, rows...  35.2 us
    pallas_call x1, Pallas kernels, on_device(): pl.pallas_call(hand_out, out_shape=tuple((jax.ShapeDtypeStruct(r.shape, r...  1.97 us

profile of v3, /device:TPU:0, one launch (start us, length us, event | category | flops | bytes accessed | tf_op | source)
XLA Modules:
  0.0 39.8 jit_solution(12420274782026780754)
XLA Ops:
  2.6 35.2 %shard_map.103 = (bf16[128,2048]{1,0:T(8,128)(2,1)}, bf16[2,128,256]{2,1,0:T(8,128)(2,1)}, bf16[2,128,256]{2,1,0:T(8,128)(2,1)}) custom-call(bf16[128,2048]{1,0:T(8,128)(2,1)} %q_hbm.1, bf16[128,2048]{1,0:T(8,128)(2,1)} %o_hbm.1, bf16[128,2048]{1,0:T(8,128)(2,1)} %do_hbm.1, bf16[2,128,256]{2,1,0:T(8,128)(2,1)} %rkv_hbm.1, bf16[2,128,256]{2,1,0:T(8,128)(2,1)} %pkv_hbm.1, ...), custom_call_target="tpu_custom_call" | custom-call | tf_op jit(solution)/shard_map/pallas_call | solution.py:336
  37.8 2.0 %shard_map.104 = (bf16[128,2048]{1,0:T(8,128)(2,1)}, bf16[2,128,256]{2,1,0:T(8,128)(2,1)}, bf16[2,128,256]{2,1,0:T(8,128)(2,1)}) custom-call(bf16[128,2048]{1,0:T(8,128)(2,1)} %get-tuple-element.6.a, bf16[2,128,256]{2,1,0:T(8,128)(2,1)} %get-tuple-element.7.b, bf16[2,128,256]{2,1,0:T(8,128)(2,1)} %get-tuple-element.8.c), custom_call_target="tpu_custom_call" | custom-call | tf_op jit(solution)/shard_map/pallas_call | solution.py:376
